TPU v7x, 32 devices: a whole 2x2x4 slice. The times are simulated.
32 devices in a mesh: band: 8 (over z, y), lev: 4 (over x, core).
Axes of the slice: x: 2, y: 2, z: 4, core: 2. Of those that a mesh axis runs over, the one named last changes fastest.
Arguments:
- obs_value: float32 [32, 8, 4, 128], P(('band', 'lev')), may hold values from -6 to 6
- obs_weight: float32 [32, 8, 4, 4, 128], P(('band', 'lev')), may hold values from 0.05 to 1
- obs_row: int32 [32, 8, 4, 128], P(('band', 'lev')), may hold values from 0 to 254, as said below
- obs_lon: int32 [32, 8, 4, 128], P(('band', 'lev')), may hold values from 0 to 1439
- obs_chan: int32 [32, 8, 4, 128], P(('band', 'lev')), may hold values from 0 to 47, as said below
- obs_count: int32 [32, 8, 4], P(('band', 'lev')), may hold values from 0 to 128, as said below
- vert_cov: float32 [4, 12, 12], replicated
- variance: float32 [4, 64], replicated, may hold values from 0.2 to 2
- quad_weight: float32 [256], P('band'), may hold values from 0.5 to 2
- legendre: bfloat16 [32, 65, 256], P('band'), may hold values from -0.375 to 0.375
Outputs:
- increment: float32 [12, 4, 256, 1440], P('lev', None, 'band')
Inputs may be any that keep to these rules, and one draw needn't show every extreme that they name: Every slot of bucket (s, b, q) has obs_row between b * 32 and (b + 1) * 32 - 1, and below 255. `obs_chan`: every slot of bucket (s, b, q) observes a level between q * 3 and (q + 1) * 3 - 1. `obs_count`: in every draw one destination bucket (b, q) is full from every source device; loads differ between destinations.
All inputs are finite; a program needn't handle non-finite values.
Results may differ from a plain program's by a relative error of at most 0.0003.
Values sent between devices are 32-bit elements; how exact they have to be, the bound alone decides.
A program may use at most 128 MiB of HBM per device.

v0:
```python
import math

import jax
import jax.numpy as jnp
from jax import lax
from jax.sharding import PartitionSpec as P

NLON = 1440


def shifted(value, axis, steps):
    count = lax.axis_size(axis)
    initial, last = (max(0, -steps), min(count, count - steps))
    return lax.ppermute(value, axis, [(source, source + steps) for source in range(initial, last)])


def phase_tables(orders, nlon):
    columns = jnp.arange(nlon, dtype=jnp.int32)
    phases = orders[None, :] * columns[:, None] % nlon
    angles = phases.astype(jnp.float32) * (2.0 * math.pi / nlon)
    return (jnp.cos(angles), jnp.sin(angles))


def analyse(legendre_part, arrived_spec, first_pair, order_total, variance):
    highest = lax.Precision.HIGHEST
    both_orders = jnp.einsum("prj,kvjphz->phrkvz", legendre_part, arrived_spec, precision=highest)
    pair_count = legendre_part.shape[0]
    pair_ids = first_pair + jnp.arange(pair_count, dtype=jnp.int32)
    row_ids = jnp.arange(order_total + 1, dtype=jnp.int32)
    low_rows = row_ids[None, :] < order_total - pair_ids[:, None]
    coefficients = jnp.where(low_rows[:, :, None, None, None], both_orders[:, 0], both_orders[:, 1])
    degree = jnp.where(low_rows, pair_ids[:, None] + row_ids[None, :], row_ids[None, :] - 1)
    onehot = (degree[..., None] == jnp.arange(order_total, dtype=jnp.int32)).astype(jnp.float32)
    row_variance = jnp.einsum("prm,vm->prv", onehot, variance, precision=highest)
    return (coefficients, row_variance, low_rows)


def synthesise(legendre_part, coefficients, row_variance, low_rows):
    scaled = coefficients * row_variance[:, :, None, :, None]
    low_mask = low_rows[:, :, None, None, None]
    split_rows = jnp.stack(
        [
            jnp.where(low_mask, scaled, jnp.float32(0.0)),
            jnp.where(low_mask, jnp.float32(0.0), scaled),
        ],
        axis=1,
    )
    return jnp.einsum(
        "prj,phrkvz->kvjphz", legendre_part, split_rows, precision=lax.Precision.HIGHEST
    )


def body(
    obs_value,
    obs_weight,
    obs_row,
    obs_lon,
    obs_chan,
    obs_count,
    vert_cov,
    variance,
    quad_weight,
    legendre,
):
    highest = lax.Precision.HIGHEST
    legendre_wide = legendre.astype(jnp.float32)
    band_count = lax.axis_size("band")
    lev_count = lax.axis_size("lev")
    band_index = lax.axis_index("band")
    level_index = lax.axis_index("lev")
    var_count = vert_cov.shape[0]
    levels = vert_cov.shape[1]
    lev_local = levels // lev_count
    lat_rows = quad_weight.shape[0]
    lat_total = lat_rows * band_count
    pair_local = legendre.shape[0]
    order_total = legendre.shape[1] - 1
    obs_values = obs_value[0]
    slot_shape = obs_values.shape
    live_rows = lax.broadcasted_iota(jnp.int32, slot_shape, 2) < obs_count[0][..., None]
    contribution = jnp.where(live_rows, obs_values, jnp.float32(0.0))[:, :, None, :] * obs_weight[0]
    dest_band = lax.broadcasted_iota(jnp.int32, slot_shape, 0)
    dest_group = lax.broadcasted_iota(jnp.int32, slot_shape, 1)
    channel = obs_chan[0]
    flat_channel = (channel % levels - dest_group * lev_local) * var_count + channel // levels
    packed = (flat_channel * lat_rows + obs_row[0] - dest_band * lat_rows) * NLON + obs_lon[0]
    arrived = lax.all_to_all(
        lax.all_to_all(contribution, "band", split_axis=0, concat_axis=0, tiled=True),
        "lev",
        split_axis=1,
        concat_axis=0,
        tiled=True,
    )
    cell_codes = lax.all_to_all(
        lax.all_to_all(packed, "band", split_axis=0, concat_axis=0, tiled=True),
        "lev",
        split_axis=1,
        concat_axis=0,
        tiled=True,
    )
    lon_index = cell_codes % NLON
    remainder = cell_codes // NLON
    row_local = remainder % lat_rows
    base_row = remainder // lat_rows * (lat_rows + 1) + row_local
    east_index = (lon_index + 1) % NLON
    targets = jnp.stack(
        [
            base_row * NLON + lon_index,
            base_row * NLON + east_index,
            (base_row + 1) * NLON + lon_index,
            (base_row + 1) * NLON + east_index,
        ],
        axis=2,
    )
    partial_value = jnp.zeros((lev_local * var_count * (lat_rows + 1) * NLON,), jnp.float32)
    partial_value = partial_value.at[targets.reshape(-1)].add(arrived.reshape(-1))
    partial_value = partial_value.reshape(lev_local, var_count, lat_rows + 1, NLON)
    incoming = shifted(partial_value[:, :, lat_rows], "band", 1)
    grid_field = partial_value[:, :, :lat_rows].at[:, :, 0].add(incoming)
    order_ids = jnp.arange(order_total, dtype=jnp.int32)
    pair_of = order_ids // 2
    forward_orders = jnp.where(order_ids % 2 == 0, pair_of, order_total - 1 - pair_of)
    cosine_table, sine_table = phase_tables(forward_orders, NLON)
    flat_grid = grid_field.reshape(-1, NLON)
    real_part = jnp.dot(flat_grid, cosine_table, precision=highest) / NLON
    imag_part = -jnp.dot(flat_grid, sine_table, precision=highest) / NLON
    spectrum = jnp.stack([real_part, imag_part], axis=-1).reshape(
        lev_local, var_count, lat_rows, order_total, 2
    )
    spectrum = spectrum * quad_weight[None, None, :, None, None]
    gathered = lax.all_to_all(spectrum, "band", split_axis=3, concat_axis=2, tiled=True)
    gathered = gathered.reshape(lev_local, var_count, lat_total, pair_local, 2, 2)
    coefficients, row_variance, low_rows = analyse(
        legendre_wide, gathered, band_index * pair_local, order_total, variance
    )
    own_rows = lax.dynamic_slice_in_dim(vert_cov, level_index * lev_local, lev_local, 1)
    mixed = jnp.einsum(
        "vkl,prlvz->prkvz",
        own_rows,
        lax.all_gather(coefficients, "lev", axis=2, tiled=True),
        precision=highest,
    )
    synthesised = synthesise(legendre_wide, mixed, row_variance, low_rows).reshape(
        lev_local, var_count, lat_total, 2 * pair_local, 2
    )
    returned = lax.all_to_all(synthesised, "band", split_axis=2, concat_axis=3, tiled=True)
    back_cosine, back_sine = phase_tables(forward_orders, NLON)
    order_factor = jnp.where(forward_orders == 0, jnp.float32(1.0), jnp.float32(2.0))
    flat_back = returned.reshape(-1, order_total, 2)
    increment = jnp.dot(flat_back[..., 0] * order_factor, back_cosine.T, precision=highest)
    increment = increment - jnp.dot(
        flat_back[..., 1] * order_factor, back_sine.T, precision=highest
    )
    return increment.reshape(lev_local, var_count, lat_rows, NLON)


def solution(mesh):
    placed = (
        P(("band", "lev"), None, None, None),
        P(("band", "lev"), None, None, None, None),
        P(("band", "lev"), None, None, None),
        P(("band", "lev"), None, None, None),
        P(("band", "lev"), None, None, None),
        P(("band", "lev"), None, None),
        P(),
        P(),
        P("band"),
        P("band", None, None),
    )
    return jax.shard_map(
        body, mesh=mesh, in_specs=placed, out_specs=P("lev", None, "band", None), check_vma=False
    )
```

profile of v0, /device:TPU:0, one launch (start us, length us, event | category | flops | bytes accessed | tf_op | source)
XLA Modules:
  0.0 215.5 jit_solution(13180083341486272452)
XLA Ops:
  1.5 7.3 %all-to-all-start = ((s32[8,4,128]{2,1,0:T(4,128)}), s32[8,4,128]{2,1,0:T(4,128)S(1)}, u32[]{:S(2)}, u32[]{:S(2)}) async-start(s32[8,4,128]{2,1,0:T(4,128)} %copy.104), calls=%async_computation | async-start | bytes 32768 | tf_op jit(solution)/shard_map/all_to_all | solution.py:95
  10.3 1.5 bitcast_multiply_fusion
  11.8 3.5 %all-to-all-done = s32[8,4,128]{2,1,0:T(4,128)S(1)} async-done(((s32[8,4,128]{2,1,0:T(4,128)}), s32[8,4,128]{2,1,0:T(4,128)S(1)}, u32[]{:S(2)}, u32[]{:S(2)}) %all-to-all-start) | async-done | bytes 16416 | tf_op jit(solution)/shard_map/all_to_all | solution.py:95
  15.9 3.2 %all-to-all-start.1 = ((s32[8,4,128]{2,0,1:T(8,128)}), s32[8,4,128]{2,0,1:T(8,128)S(1)}, u32[]{:S(2)}, u32[]{:S(2)}) async-start(s32[8,4,128]{2,0,1:T(8,128)} %copy.105), calls=%async_computation.1 | async-start | bytes 32768 | tf_op jit(solution)/shard_map/all_to_all | solution.py:94
  19.3 3.7 %all-to-all-done.1 = s32[8,4,128]{2,0,1:T(8,128)S(1)} async-done(((s32[8,4,128]{2,0,1:T(8,128)}), s32[8,4,128]{2,0,1:T(8,128)S(1)}, u32[]{:S(2)}, u32[]{:S(2)}) %all-to-all-start.1) | async-done | bytes 16416 | tf_op jit(solution)/shard_map/all_to_all | solution.py:94
  23.0 3.4 %all-to-all-start.2 = ((f32[8,4,4,128]{3,2,1,0:T(4,128)}), f32[8,4,4,128]{3,2,1,0:T(4,128)S(1)}, u32[]{:S(2)}, u32[]{:S(2)}) async-start(f32[8,4,4,128]{3,2,1,0:T(4,128)} %bitcast_multiply_fusion), calls=%async_computation.2 | async-start | bytes 131072 | tf_op jit(solution)/shard_map/all_to_all | solution.py:88
  26.5 6.7 %all-to-all-done.2 = f32[8,4,4,128]{3,2,1,0:T(4,128)S(1)} async-done(((f32[8,4,4,128]{3,2,1,0:T(4,128)}), f32[8,4,4,128]{3,2,1,0:T(4,128)S(1)}, u32[]{:S(2)}, u32[]{:S(2)}) %all-to-all-start.2) | async-done | bytes 65568 | tf_op jit(solution)/shard_map/all_to_all | solution.py:88
  33.8 3.3 %all-to-all-start.3 = ((f32[8,4,4,128]{3,2,0,1:T(4,128)}), f32[8,4,4,128]{3,2,0,1:T(4,128)S(1)}, u32[]{:S(2)}, u32[]{:S(2)}) async-start(f32[8,4,4,128]{3,2,0,1:T(4,128)} %copy.108), calls=%async_computation.3 | async-start | bytes 131072 | tf_op jit(solution)/shard_map/all_to_all | solution.py:87
  37.2 4.0 %all-to-all-done.3 = f32[8,4,4,128]{3,2,0,1:T(4,128)S(1)} async-done(((f32[8,4,4,128]{3,2,0,1:T(4,128)}), f32[8,4,4,128]{3,2,0,1:T(4,128)S(1)}, u32[]{:S(2)}, u32[]{:S(2)}) %all-to-all-start.3) | async-done | bytes 65568 | tf_op jit(solution)/shard_map/all_to_all | solution.py:87
  41.2 87.3 %scatter_custom_fusion = f32[570240]{0:T(1024)} fusion(s32[16384]{0:T(1024)S(1)} %bitcast.191, f32[16384]{0:T(1024)S(1)} %bitcast.190, f32[]{:T(128)} %constant.149.clone.1), kind=kCustom, calls=%fused_computation.2 | custom fusion | flops 16384 | bytes 2280964 | tf_op jit(solution)/shard_map/scatter-add | solution.py:116
  128.5 3.3 %reshape.529 = f32[3,4,33,1440]{3,2,1,0:T(8,128)S(1)} reshape(f32[570240]{0:T(1024)} %scatter_custom_fusion) | data formatting | bytes 4561920 | tf_op jit(solution)/shard_map/reshape | solution.py:117
  131.9 2.5 %collective-permute-start = (f32[3,4,1440]{2,1,0:T(4,128)S(1)}, f32[3,4,1440]{2,1,0:T(4,128)S(1)}, u32[]{:S(2)}, u32[]{:S(2)}) collective-permute-start(f32[3,4,1440]{2,1,0:T(4,128)S(1)} %bitcast.189), channel_id=1, source_target_pairs={{0,4},{4,8},{8,12},{12,16},{16,20},{20,24},{24,28},{1,5},{5,9},{9,... | collective-permute-start | bytes 207368 | tf_op jit(solution)/shard_map/ppermute | solution.py:14
  134.4 1.9 slice.53
  136.5 1.3 scatter-add.13
  137.8 5.2 %convolution_multiply_fusion = f32[384,64]{0,1:T(8,128)S(1)} fusion(f32[384,1440]{1,0:T(8,128)S(1)} %bitcast.177, s32[64]{0:T(128)S(1)} %compare_select_fusion.2), kind=kOutput, calls=%fused_computation.7 | convolution fusion | flops 425527296 | bytes 2310400 | tf_op jit(solution)/shard_map/dot_general | solution.py:125
  143.0 5.2 %fusion.2 = f32[384,64]{0,1:T(8,128)S(1)} fusion(f32[384,1440]{1,0:T(8,128)S(1)} %bitcast.178, s32[64]{0:T(128)S(1)} %compare_select_fusion.2), kind=kOutput, calls=%fused_computation.6 | convolution fusion | flops 425551872 | bytes 2310400 | tf_op jit(solution)/shard_map/dot_general | solution.py:126
  149.0 1.2 reshape.550
  150.2 4.8 %all-to-all-start.4 = ((f32[8,1,6144]{2,1,0:T(1,128)}), f32[8,1,6144]{2,1,0:T(1,128)S(1)}, u32[]{:S(2)}, u32[]{:S(2)}) async-start(f32[8,1,6144]{2,1,0:T(1,128)} %reshape.550), calls=%async_computation.4 | async-start | bytes 393216 | tf_op jit(solution)/shard_map/all_to_all | solution.py:131
  155.9 6.8 %all-to-all-done.4 = f32[8,1,6144]{2,1,0:T(1,128)S(1)} async-done(((f32[8,1,6144]{2,1,0:T(1,128)}), f32[8,1,6144]{2,1,0:T(1,128)S(1)}, u32[]{:S(2)}, u32[]{:S(2)}) %all-to-all-start.4) | async-done | bytes 196640 | tf_op jit(solution)/shard_map/all_to_all | solution.py:131
  163.3 1.1 reduce.2
  165.9 5.6 %all_gather.3 = f32[4,65,12,4,2]{1,3,4,2,0:T(4,128)S(1)} all-gather(f32[4,65,3,4,2]{1,3,4,2,0:T(4,128)S(1)} %fusion.44), channel_id=1, replica_groups=mesh['band'=8,'lev'=4] {'lev'}, dimensions={2}, use_global_device_ids=true | all-gather | bytes 124800 | tf_op jit(solution)/shard_map/all_gather | solution.py:140
  172.1 2.2 %copy.124 = f32[3,4,256,8,2]{3,4,1,0,2:T(2,128)S(1)} copy(f32[3,4,256,8,2]{2,1,4,0,3:T(4,128)S(1)} %bitcast.185) | data formatting | bytes 393216 | tf_op jit(solution)/shard_map/reshape | solution.py:143
  174.3 5.7 %reshape.552 = f32[8,1,6144]{2,1,0:T(1,128)} reshape(f32[256,3,4,2,8]{4,3,2,1,0:T(2,128)S(1)} %bitcast.179) | data formatting | bytes 393216
  180.0 3.4 %all-to-all-start.5 = ((f32[8,1,6144]{2,1,0:T(1,128)}), f32[8,1,6144]{2,1,0:T(1,128)S(1)}, u32[]{:S(2)}, u32[]{:S(2)}) async-start(f32[8,1,6144]{2,1,0:T(1,128)} %reshape.552), calls=%async_computation.5 | async-start | bytes 393216 | tf_op jit(solution)/shard_map/all_to_all | solution.py:146
  183.5 8.7 %all-to-all-done.5 = f32[8,1,6144]{2,1,0:T(1,128)S(1)} async-done(((f32[8,1,6144]{2,1,0:T(1,128)}), f32[8,1,6144]{2,1,0:T(1,128)S(1)}, u32[]{:S(2)}, u32[]{:S(2)}) %all-to-all-start.5) | async-done | bytes 196640 | tf_op jit(solution)/shard_map/all_to_all | solution.py:146
  192.1 1.1 reduce.3
  193.2 4.8 %reshape.553 = f32[256,3,4,2,8]{4,3,2,1,0:T(2,128)S(1)} reshape(f32[8,6144]{1,0:T(8,128)S(1)} %reduce.3) | data formatting | bytes 393216
  198.0 3.4 %copy.135 = f32[3,4,8,32,8,2]{3,2,4,5,1,0:T(8,128)} copy(f32[3,4,8,32,8,2]{4,5,1,0,3,2:T(2,128)S(1)} %bitcast.180) | data formatting | bytes 393216 | tf_op jit(solution)/shard_map/all_to_all | solution.py:146
  201.4 1.6 copy.126
  203.5 4.7 %fusion.9 = f32[384,1440]{0,1:T(8,128)S(1)} fusion(s32[64]{0:T(128)S(1)} %compare_select_fusion.2, f32[384,64,2]{0,1,2:T(8,128)S(1)} %reshape.534, f32[64]{0:T(128)S(1)} %compare_select_fusion.1), kind=kOutput, calls=%fused_computation.17 | convolution fusion | flops 425527296 | bytes 2311168 | tf_op jit(solution)/shard_map/dot_general | solution.py:150
  208.1 4.8 %convolution_subtract_fusion = f32[384,1440]{0,1:T(8,128)S(1)} fusion(f32[384,1440]{0,1:T(8,128)S(1)} %fusion.9, s32[64]{0:T(128)S(1)} %compare_select_fusion.2, f32[384,64,2]{0,1,2:T(8,128)S(1)} %reshape.534, f32[64]{0:T(128)S(1)} %compare_select_fusion.1), kind=kOutput, calls=%fused_computation.1 | convolution fusion | flops 426080256 | bytes 4523008 | tf_op jit(solution)/shard_map/dot_general | solution.py:151
  212.9 2.1 copy.127
  (48 shorter events, 9.4 us)
Async XLA Ops:
  0.0 165.4 %copy-start = (bf16[4,65,256]{2,0,1:T(4,128)(2,1)S(1)}, bf16[4,65,256]{2,0,1:T(4,128)(2,1)}, u32[]{:S(2)}) copy-start(bf16[4,65,256]{2,0,1:T(4,128)(2,1)} %param.21) | copy-start | bytes 399364
  1.5 13.9 %all-to-all-start = ((s32[8,4,128]{2,1,0:T(4,128)}), s32[8,4,128]{2,1,0:T(4,128)S(1)}, u32[]{:S(2)}, u32[]{:S(2)}) async-start(s32[8,4,128]{2,1,0:T(4,128)} %copy.104), calls=%async_computation | async-start | bytes 32768 | tf_op jit(solution)/shard_map/all_to_all | solution.py:95
  15.9 7.1 %all-to-all-start.1 = ((s32[8,4,128]{2,0,1:T(8,128)}), s32[8,4,128]{2,0,1:T(8,128)S(1)}, u32[]{:S(2)}, u32[]{:S(2)}) async-start(s32[8,4,128]{2,0,1:T(8,128)} %copy.105), calls=%async_computation.1 | async-start | bytes 32768 | tf_op jit(solution)/shard_map/all_to_all | solution.py:94
  23.0 10.2 %all-to-all-start.2 = ((f32[8,4,4,128]{3,2,1,0:T(4,128)}), f32[8,4,4,128]{3,2,1,0:T(4,128)S(1)}, u32[]{:S(2)}, u32[]{:S(2)}) async-start(f32[8,4,4,128]{3,2,1,0:T(4,128)} %bitcast_multiply_fusion), calls=%async_computation.2 | async-start | bytes 131072 | tf_op jit(solution)/shard_map/all_to_all | solution.py:88
  33.8 7.4 %all-to-all-start.3 = ((f32[8,4,4,128]{3,2,0,1:T(4,128)}), f32[8,4,4,128]{3,2,0,1:T(4,128)S(1)}, u32[]{:S(2)}, u32[]{:S(2)}) async-start(f32[8,4,4,128]{3,2,0,1:T(4,128)} %copy.108), calls=%async_computation.3 | async-start | bytes 131072 | tf_op jit(solution)/shard_map/all_to_all | solution.py:87
  131.8 2.6 %copy-start.1 = (f32[3,4,33,1440]{3,2,1,0:T(8,128)}, f32[3,4,33,1440]{3,2,1,0:T(8,128)S(1)}, u32[]{:S(2)}) copy-start(f32[3,4,33,1440]{3,2,1,0:T(8,128)S(1)} %reshape.529) | copy-start | bytes 6842884
  131.9 4.4 %collective-permute-start = (f32[3,4,1440]{2,1,0:T(4,128)S(1)}, f32[3,4,1440]{2,1,0:T(4,128)S(1)}, u32[]{:S(2)}, u32[]{:S(2)}) collective-permute-start(f32[3,4,1440]{2,1,0:T(4,128)S(1)} %bitcast.189), channel_id=1, source_target_pairs={{0,4},{4,8},{8,12},{12,16},{16,20},{20,24},{24,28},{1,5},{5,9},{9,... | collective-permute-start | bytes 207368 | tf_op jit(solution)/shard_map/ppermute | solution.py:14
  137.8 10.7 %copy-start.2 = (f32[32]{0:T(128)S(1)}, f32[32]{0:T(128)}, u32[]{:S(2)}) copy-start(f32[32]{0:T(128)} %param.20) | copy-start | bytes 388
  148.2 7.5 %copy-start.3 = (f32[4,64]{1,0:T(4,128)S(1)}, f32[4,64]{1,0:T(4,128)}, u32[]{:S(2)}) copy-start(f32[4,64]{1,0:T(4,128)} %param.19) | copy-start | bytes 3076
  150.2 12.5 %all-to-all-start.4 = ((f32[8,1,6144]{2,1,0:T(1,128)}), f32[8,1,6144]{2,1,0:T(1,128)S(1)}, u32[]{:S(2)}, u32[]{:S(2)}) async-start(f32[8,1,6144]{2,1,0:T(1,128)} %reshape.550), calls=%async_computation.4 | async-start | bytes 393216 | tf_op jit(solution)/shard_map/all_to_all | solution.py:131
  180.0 12.1 %all-to-all-start.5 = ((f32[8,1,6144]{2,1,0:T(1,128)}), f32[8,1,6144]{2,1,0:T(1,128)S(1)}, u32[]{:S(2)}, u32[]{:S(2)}) async-start(f32[8,1,6144]{2,1,0:T(1,128)} %reshape.552), calls=%async_computation.5 | async-start | bytes 393216 | tf_op jit(solution)/shard_map/all_to_all | solution.py:146
where the time goes:
time: 220 us; the launch traced here: 215 us
  other arithmetic  93.1 us (42%)
  local copies, waits for them, and re-layouts  33.6 us (15%)
  waiting for transfers between devices  33.5 us (15%)
  starting transfers between devices  27.8 us (13%)
  matrix products  21 us (10%)
  blocking collectives  5.61 us (3%)
    scatter-add x1, other arithmetic, body(): partial_value.at[targets.reshape(-1)].add(arrived.reshape(-1))  87.3 us
    unnamed x13, local copies, waits for them, and re-layouts  12.1 us
    all_to_all x1, waiting for transfers between devices, body(): lax.all_to_all(synthesised, 'band', split_axis=2, concat_axis=3, tiled=True)  8.67 us
    all_to_all x1, starting transfers between devices, body(): lax.all_to_all(packed, 'band', split_axis=0, concat_axis=0, tiled=True)  7.29 us
    all_to_all x1, waiting for transfers between devices, body(): lax.all_to_all(spectrum, 'band', split_axis=3, concat_axis=2, tiled=True)  6.82 us
    all_to_all x1, waiting for transfers between devices, body(): lax.all_to_all(contribution, 'band', split_axis=0, concat_axis=0, tiled=T...  6.71 us
    all_gather x1, blocking collectives, body(): lax.all_gather(coefficients, 'lev', axis=2, tiled=True)  5.61 us
    dot_general x1, matrix products, body(): imag_part = -jnp.dot(flat_grid, sine_table, precision=highest) / NLON  5.23 us
  transfers between devices with their start and end apart: 7, of which 6 were waited for; matrix products, arithmetic and copies ran while one was open for 3% of the time, Pallas kernels for 0%

commit v1 on v0

v1 whole, which is shorter than its diff:
```python
import functools
import math

import jax
import jax.numpy as jnp
import ml_dtypes
import numpy as np
from jax import lax
from jax.experimental import pallas as pl
from jax.experimental.pallas import tpu as pltpu
from jax.sharding import PartitionSpec as P

NLON = 1440
FINE = 32
COARSE = 48
MESH = pl.DeviceIdType.MESH
LANES = 128
NT = (((1,), (1,)), ((), ()))
NN = (((1,), (0,)), ((), ()))


def split_np(table, parts):
    out = []
    rest = np.asarray(table, np.float64)
    for _ in range(parts):
        piece = rest.astype(np.float32).astype(ml_dtypes.bfloat16)
        out.append(piece)
        rest = rest - piece.astype(np.float64)
    return out


def row_orders(orders):
    pairs = np.arange(orders // 2)
    four = np.stack([pairs, pairs, orders - 1 - pairs, orders - 1 - pairs], axis=1).reshape(-1)
    is_sine = np.tile(np.array([0, 1, 0, 1]), orders // 2)
    return four, is_sine


def point_table(orders):
    order, is_sine = row_orders(orders)
    unit = 2.0 * math.pi / NLON
    coarse = (order[:, None] * FINE * np.arange(COARSE)[None, :] % NLON) * unit + is_sine[:, None] * (math.pi / 2)
    fine = (order[:, None] * np.arange(FINE)[None, :] % NLON) * unit
    east = (order[:, None] * (np.arange(FINE) + 1)[None, :] % NLON) * unit
    no_a, no_b = np.zeros_like(coarse), np.zeros_like(fine)
    rows = [
        np.concatenate([np.cos(coarse), no_b], 1),
        np.concatenate([np.sin(coarse), no_b], 1),
        np.concatenate([no_a, np.cos(fine)], 1),
        np.concatenate([no_a, np.sin(fine)], 1),
        np.concatenate([no_a, np.cos(east)], 1),
        np.concatenate([no_a, np.sin(east)], 1),
    ]
    parts = split_np(np.concatenate(rows, 0), 3)
    pad = np.zeros((parts[0].shape[0], 256 - 3 * (COARSE + FINE)), ml_dtypes.bfloat16)
    return np.concatenate(parts + [pad], 1)


def back_table(orders):
    order, is_sine = row_orders(orders)
    angle = (order[:, None] * np.arange(NLON)[None, :] % NLON) * (2.0 * math.pi / NLON)
    factor = np.where(order == 0, 1.0, 2.0)[:, None] / NLON
    table = factor * np.where(is_sine[:, None] == 1, -np.sin(angle), np.cos(angle))
    table = np.repeat(table.reshape(-1, 1, 4, NLON), 2, axis=1).reshape(-1, NLON)
    high, low = split_np(table, 2)
    return high, low


def observation_group(devices):
    return 4 if devices <= 64 else 1


def two(value):
    high = value.astype(jnp.bfloat16)
    low = (value - high.astype(jnp.float32)).astype(jnp.bfloat16)
    return high, low


def dot2(value, weights, dims):
    count = value.shape[0]
    both = jnp.concatenate(list(two(value)), axis=0)
    out = lax.dot_general(both, weights, dims, preferred_element_type=jnp.float32)
    return out[:count] + out[count:]


def main_kernel(
    nb, nl, levels,
    val_ref, wgt_ref, row_ref, lon_ref, chan_ref, cnt_ref, cov_ref, var_ref, quad_ref, leg_ref, tab_ref,
    out_ref,
    send1, recv1, send2, recv2, send3, recv3, acc, lpad, xbuf, ssem, rsem1, rsem2, rsem3,
):
    devices = nb * nl
    band, lev = lax.axis_index("band"), lax.axis_index("lev")
    me = band * nl + lev
    lev_local = levels // nl
    var_count = cov_ref.shape[0]
    rows2 = acc.shape[0] // 2
    orders = leg_ref.shape[1] - 1
    nj = leg_ref.shape[2]
    rp = lpad.shape[0]
    tiles = nj // LANES
    per1 = observation_group(devices)
    groups = devices // per1
    highest = lax.Precision.HIGHEST

    barrier = pltpu.get_barrier_semaphore()

    def greet(k, c):
        d = lax.rem(me + k, devices)
        pl.semaphore_signal(barrier, inc=1, device_id=(d // nl, lax.rem(d, nl)), device_id_type=MESH)
        return c

    lax.fori_loop(1, devices, greet, 0)

    slot = lax.broadcasted_iota(jnp.int32, (1, LANES), 1)

    def pack(b, c):
        for q in range(nl):
            d = b * nl + q
            live = slot < cnt_ref[b, q]
            value = jnp.where(live, val_ref[b, pl.ds(q, 1), :], 0.0)
            send1[d, 0:4, :] = value * wgt_ref[b, q]
            chan = chan_ref[b, pl.ds(q, 1), :]
            variable = jnp.where(chan >= levels, 1, 0)
            for v in range(2, var_count):
                variable = variable + jnp.where(chan >= v * levels, 1, 0)
            level = chan - variable * levels - q * lev_local
            target = (level * var_count + variable) * 32 + row_ref[b, pl.ds(q, 1), :] - b * 32
            send1[d, 4:5, :] = target.astype(jnp.float32)
            send1[d, 5:6, :] = lon_ref[b, pl.ds(q, 1), :].astype(jnp.float32)
            send1[d, 6:7, :] = quad_ref[...]
            send1[d, 7:8, :] = jnp.zeros((1, LANES), jnp.float32)
        return c

    lax.fori_loop(0, nb, pack, 0)
    pl.semaphore_wait(barrier, devices - 1)

    def scatter_out(send, recv, phase, rsem, per):
        def one(k, c):
            d = lax.rem(me + k, devices)
            pltpu.make_async_remote_copy(
                src_ref=send.at[d],
                dst_ref=recv.at[me],
                send_sem=ssem.at[phase],
                recv_sem=rsem.at[me // per],
                device_id=(d // nl, lax.rem(d, nl)),
                device_id_type=MESH,
            ).start()
            return c

        pltpu.make_async_copy(send.at[me], recv.at[me], rsem.at[me // per]).start()
        lax.fori_loop(1, devices, one, 0)

    def wait_group(recv, rsem, index, per):
        part = recv.at[pl.ds(index * per, per)]
        pltpu.make_async_copy(part, part, rsem.at[index]).wait()

    def wait_sent(send, phase):
        part = send.at[pl.ds(0, devices - 1)]
        pltpu.make_async_copy(part, part, ssem.at[phase]).wait()

    scatter_out(send1, recv1, 0, rsem1, per1)

    acc[...] = jnp.zeros_like(acc)
    lpad[...] = jnp.zeros_like(lpad)
    lpad[0:orders + 1, :] = leg_ref[lev].astype(jnp.float32)
    leg = lpad[...].astype(jnp.bfloat16)

    degree_r = lax.broadcasted_iota(jnp.int32, (orders, rp), 1)
    degree_d = lax.broadcasted_iota(jnp.int32, (orders, rp), 0)
    degree = jnp.where(degree_r < orders - me, me + degree_r, degree_r - 1)
    row_var = lax.dot_general(
        var_ref[...], jnp.where(degree == degree_d, 1.0, 0.0), NN, precision=highest, preferred_element_type=jnp.float32
    )

    per_v = nl * 16
    mr = lax.broadcasted_iota(jnp.int32, (per_v, levels), 0)
    ml = lax.broadcasted_iota(jnp.int32, (per_v, levels), 1)
    tau = (mr % 16) // 4
    expand = jnp.where((tau < lev_local) & (ml == (mr // 16) * lev_local + tau), 1.0, 0.0)
    same = lax.broadcasted_iota(jnp.int32, (per_v, per_v), 0) % 4 == lax.broadcasted_iota(jnp.int32, (per_v, per_v), 1) % 4
    mixers = []
    for v in range(var_count):
        left = lax.dot_general(expand, cov_ref[v], NN, precision=highest, preferred_element_type=jnp.float32)
        full = lax.dot_general(left, expand, NT, precision=highest, preferred_element_type=jnp.float32)
        mixers.append(jnp.where(same, full, 0.0))

    target_ids = lax.broadcasted_iota(jnp.int32, (3 * LANES, LANES), 0).astype(jnp.float32)
    coarse_ids = lax.broadcasted_iota(jnp.int32, (COARSE, LANES), 0)
    fine_ids = lax.broadcasted_iota(jnp.int32, (FINE, LANES), 0)

    def gather_obs(index, c):
        wait_group(recv1, rsem1, index, per1)
        hots, picks = [], []
        for g in range(per1):
            s = index * per1 + g
            hots.append(jnp.where(target_ids == recv1[s, 4:5, :], 1.0, 0.0).astype(jnp.bfloat16))
            lon = recv1[s, 5:6, :].astype(jnp.int32)
            a = jnp.where(coarse_ids == lon // FINE, 1.0, 0.0).astype(jnp.bfloat16)
            b = jnp.where(fine_ids == lon % FINE, 1.0, 0.0).astype(jnp.bfloat16)
            picks.append(jnp.concatenate([a, b, a, b, a, b, jnp.zeros((16, LANES), jnp.bfloat16)], axis=0))
        hot = jnp.concatenate(hots, axis=1)
        pick = jnp.concatenate(picks, axis=1)
        trig = lax.dot_general(tab_ref[...], pick, NN, preferred_element_type=jnp.float32)
        ca, sa, cb, sb, ce, se = [trig[i * rows2:(i + 1) * rows2] for i in range(6)]
        here = ca * cb - sa * sb
        east = ca * ce - sa * se
        weights = [
            jnp.concatenate([recv1[index * per1 + g, k:k + 1, :] for g in range(per1)], axis=1) for k in range(4)
        ]
        first = here * weights[0] + east * weights[1]
        second = here * weights[2] + east * weights[3]
        acc[...] += dot2(jnp.concatenate([first, second], axis=0), hot, NT)
        return c

    lax.fori_loop(0, groups, gather_obs, 0)

    lane2 = lax.broadcasted_iota(jnp.int32, (rows2, LANES), 1) % 32
    sub2 = lax.broadcasted_iota(jnp.int32, (rows2, LANES), 0) % 8
    spec = []
    halo = jnp.zeros((rows2, LANES), jnp.float32)
    for t in range(lev_local):
        columns = slice(t * LANES, (t + 1) * LANES)
        north = acc[rows2:, columns]
        spec.append(acc[0:rows2, columns] + jnp.where(lane2 >= 1, pltpu.roll(north, 1, 1), 0.0))
        halo = halo + jnp.where(lane2 == t, pltpu.roll(north, (t - 31) % LANES, 1), 0.0)
    spec.append(halo)
    for h in range(2):
        s0, s1 = spec[2 * h], spec[2 * h + 1]
        even = jnp.where(sub2 < 4, s0, pltpu.roll(s1, 4, 0)).reshape(rows2 // 8, 8, LANES)
        odd = jnp.where(sub2 < 4, pltpu.roll(s0, rows2 - 4, 0), s1).reshape(rows2 // 8, 8, LANES)
        for i in range(rows2 // 8):
            send2[2 * i, h] = even[i]
            send2[2 * i + 1, h] = odd[i]
    per2 = 4 * nl
    scatter_out(send2, recv2, 1, rsem2, per2)

    group_of = lax.broadcasted_iota(jnp.int32, (8, LANES), 1) // 32
    quads = []
    for jt in range(tiles):
        tile = jnp.zeros((8, LANES), jnp.float32)
        for beta in range(4):
            row = jnp.broadcast_to(recv1[(4 * jt + beta) * nl, 6:7, :], (8, LANES))
            tile = jnp.where(group_of == beta, row, tile)
        quads.append(tile)
    quad = jnp.concatenate(quads, axis=1)
    lane_j = lax.broadcasted_iota(jnp.int32, (8, nj), 1) % 32
    quad_next = jnp.zeros((8, nj), jnp.float32)
    for t in range(lev_local):
        quad_next = jnp.where(lane_j == t, pltpu.roll(quad, nj - 32 + t, 1), quad_next)
    lane_r = lax.broadcasted_iota(jnp.int32, (rp, nj), 1) % 32
    cross = []
    for t in range(lev_local):
        cross.append(jnp.where(lane_r == t, pltpu.roll(lpad[...], nj - 32 + t, 1), 0.0).astype(jnp.bfloat16))
    cross = jnp.concatenate(cross, axis=0)
    sub16 = lax.broadcasted_iota(jnp.int32, (per_v, LANES), 0) % 16
    lane_group = lax.broadcasted_iota(jnp.int32, (per_v, LANES), 1) // 32

    for jt in range(tiles):
        wait_group(recv2, rsem2, jt, per2)
        own = jnp.broadcast_to(quad[0:1, jt * LANES:(jt + 1) * LANES], (per_v, LANES))
        nxt = jnp.broadcast_to(quad_next[0:1, jt * LANES:(jt + 1) * LANES], (per_v, LANES))
        factor = jnp.where(sub16 >= 12, nxt, own)
        blocks = [
            recv2[(4 * jt + beta) * nl:(4 * jt + beta + 1) * nl].reshape(per_v, LANES) for beta in range(4)
        ]
        for g in range(4):
            tile = jnp.zeros((per_v, LANES), jnp.float32)
            for beta in range(4):
                turned = pltpu.roll(blocks[beta], 32 * (beta - g) % LANES, 1) if beta != g else blocks[beta]
                tile = jnp.where(lane_group == beta, turned, tile)
            xbuf[g * per_v:(g + 1) * per_v, jt * LANES:(jt + 1) * LANES] = tile * factor

    xs = xbuf[...]
    coef = dot2(xs, leg, NT)
    halves = var_count * nl
    crossing = dot2(xs.reshape(halves, 2, 8, nj)[:, 1].reshape(halves * 8, nj), cross, NT)
    c0, c1, c2 = [crossing[:, t * rp:(t + 1) * rp] for t in range(3)]
    sub_h = lax.broadcasted_iota(jnp.int32, (halves * 8, rp), 0) % 8
    up = halves * 8 - 4
    add0 = jnp.where(sub_h < 4, pltpu.roll(c0, up, 0), c1).reshape(halves, 8, rp)
    add1 = pltpu.roll(c2, up, 0).reshape(halves, 8, rp)
    r_id = lax.broadcasted_iota(jnp.int32, (1, 8, rp), 2)
    s_id = lax.broadcasted_iota(jnp.int32, (1, 8, rp), 1)
    low = r_id < orders - me
    keep0 = low == (s_id % 4 < 2)
    keep1 = keep0 & (s_id < 4)
    coef = coef.reshape(halves, 2, 8, rp)
    t0 = jnp.where(keep0, coef[:, 0] + add0, 0.0)
    t1 = jnp.where(keep1, coef[:, 1] + add1, 0.0)
    coef = jnp.stack([t0, t1], axis=1).reshape(var_count * per_v, rp)
    mixed = []
    for v in range(var_count):
        scaled = coef[v * per_v:(v + 1) * per_v] * row_var[v:v + 1]
        mixed.append(
            lax.dot_general(mixers[v], scaled, NN, precision=highest, preferred_element_type=jnp.float32)
        )
    synth = dot2(jnp.concatenate(mixed, axis=0), leg, NN)

    for jt in range(tiles):
        for beta in range(4):
            tile = jnp.zeros((per_v, LANES), jnp.float32)
            for g in range(4):
                part = synth[g * per_v:(g + 1) * per_v, jt * LANES:(jt + 1) * LANES]
                turned = pltpu.roll(part, 32 * (g - beta) % LANES, 1) if beta != g else part
                tile = jnp.where(lane_group == g, turned, tile)
            send3[(4 * jt + beta) * nl:(4 * jt + beta + 1) * nl] = tile.reshape(nl, 2, 8, LANES)
    scatter_out(send3, recv3, 2, rsem3, devices)
    wait_group(recv3, rsem3, 0, devices)
    out_ref[...] = recv3[...]
    wait_sent(send1, 0)
    wait_sent(send2, 1)
    wait_sent(send3, 2)


def back_kernel(spec_ref, high_ref, low_ref, out_ref):
    level = pl.program_id(0)
    count = spec_ref.shape[0]
    sub = lax.broadcasted_iota(jnp.int32, (count * 8, LANES), 0) % 8
    block = spec_ref[:, level // 2].reshape(count * 8, LANES)
    block = jnp.where(sub // 4 == level % 2, block, 0.0)
    high, low = two(block.T)
    both = jnp.concatenate([high, low], axis=0)
    out = lax.dot_general(both, high_ref[...], NN, preferred_element_type=jnp.float32)
    rest = lax.dot_general(high, low_ref[...], NN, preferred_element_type=jnp.float32)
    out = out[:LANES] + out[LANES:] + rest
    out_ref[...] = out.reshape(out_ref.shape)


def solution(mesh):
    nb, nl = mesh.shape["band"], mesh.shape["lev"]
    devices = nb * nl

    def body(obs_value, obs_weight, obs_row, obs_lon, obs_chan, obs_count, vert_cov, variance, quad_weight, legendre):
        var_count, levels = vert_cov.shape[:2]
        lev_local = levels // nl
        lat_rows = quad_weight.shape[0]
        pair_local, order_rows, nj = legendre.shape
        orders = order_rows - 1
        assert pair_local == nl and lat_rows == 32 and var_count == 4 and lev_local == 3
        assert orders * 2 == 4 * devices and obs_value.shape[-1] == LANES
        rp = -(-order_rows // LANES) * LANES
        vmem = pl.BlockSpec(memory_space=pltpu.VMEM)
        smem = pl.BlockSpec(memory_space=pltpu.SMEM)
        block = (devices, 2, 8, LANES)
        spec = pl.pallas_call(
            functools.partial(main_kernel, nb, nl, levels),
            out_shape=jax.ShapeDtypeStruct(block, jnp.float32),
            in_specs=[vmem] * 5 + [smem] + [vmem] * 5,
            out_specs=vmem,
            scratch_shapes=[
                pltpu.VMEM((devices, 8, LANES), jnp.float32),
                pltpu.VMEM((devices, 8, LANES), jnp.float32),
                pltpu.VMEM(block, jnp.float32),
                pltpu.VMEM(block, jnp.float32),
                pltpu.VMEM(block, jnp.float32),
                pltpu.VMEM(block, jnp.float32),
                pltpu.VMEM((4 * orders, 3 * LANES), jnp.float32),
                pltpu.VMEM((rp, nj), jnp.float32),
                pltpu.VMEM((var_count * nl * 16, nj), jnp.float32),
                pltpu.SemaphoreType.DMA((3,)),
                pltpu.SemaphoreType.DMA((devices // observation_group(devices),)),
                pltpu.SemaphoreType.DMA((nj // LANES,)),
                pltpu.SemaphoreType.DMA((1,)),
            ],
            compiler_params=pltpu.CompilerParams(
                collective_id=0, has_side_effects=True, vmem_limit_bytes=56 * 2**20
            ),
            name="spectral_covariance",
        )(
            obs_value[0], obs_weight[0], obs_row[0], obs_lon[0], obs_chan[0], obs_count[0], vert_cov, variance,
            jnp.tile(quad_weight, 4)[None], legendre, jnp.asarray(point_table(orders)),
        )
        high, low = back_table(orders)
        return pl.pallas_call(
            back_kernel,
            grid=(lev_local,),
            out_shape=jax.ShapeDtypeStruct((lev_local, var_count, lat_rows, NLON), jnp.float32),
            in_specs=[
                pl.BlockSpec(block, lambda i: (0, 0, 0, 0)),
                pl.BlockSpec(high.shape, lambda i: (0, 0)),
                pl.BlockSpec(low.shape, lambda i: (0, 0)),
            ],
            out_specs=pl.BlockSpec((1, var_count, lat_rows, NLON), lambda i: (i, 0, 0, 0)),
            compiler_params=pltpu.CompilerParams(vmem_limit_bytes=56 * 2**20),
            name="inverse_transform",
        )(spec, jnp.asarray(high), jnp.asarray(low))

    placed = (
        P(("band", "lev"), None, None, None),
        P(("band", "lev"), None, None, None, None),
        P(("band", "lev"), None, None, None),
        P(("band", "lev"), None, None, None),
        P(("band", "lev"), None, None, None),
        P(("band", "lev"), None, None),
        P(),
        P(),
        P("band"),
        P("band", None, None),
    )
    return jax.shard_map(
        body, mesh=mesh, in_specs=placed, out_specs=P("lev", None, "band", None), check_vma=False
    )
```

time: 220 us -> 45.8 us (0.21); the launches traced: 215 us -> 45.5 us
  other arithmetic: 93.1 us -> 0 us
  Pallas kernels: 0 us -> 39.9 us
  waiting for transfers between devices: 33.5 us -> 0 us
  local copies, waits for them, and re-layouts: 33.6 us -> 5.6 us
  starting transfers between devices: 27.8 us -> 0 us
  matrix products: 21 us -> 0 us
  blocking collectives: 5.61 us -> 0 us
    scatter-add x1 -> x0, other arithmetic: 87.3 us -> none  [body(): partial_value.at[targets.reshape(-1)].add(arrived.reshape(-1))]
    pallas_call x0 -> x2, Pallas kernels: none -> 39.9 us  [the longest x1 35.6 us: body(): pl.pallas_call(functools.partial(main_kernel, nb, nl, levels), out_shape=...]
    all_to_all x6 -> x0, waiting for transfers between devices: 33.5 us -> none  [the longest x1 8.67 us: body(): lax.all_to_all(synthesised, 'band', split_axis=2, concat_axis=3, tiled=True)]
    all_to_all x6 -> x0, starting transfers between devices: 25.3 us -> none  [the longest x1 7.29 us: body(): lax.all_to_all(packed, 'band', split_axis=0, concat_axis=0, tiled=True)]
    dot_general x8 -> x0, matrix products: 21 us -> none  [the longest x1 5.23 us: body(): imag_part = -jnp.dot(flat_grid, sine_table, precision=highest) / NLON]
    unnamed x13 -> x2, local copies, waits for them, and re-layouts: 12.1 us -> 2.92 us
    all_to_all x7 -> x0, local copies, waits for them, and re-layouts: 7.07 us -> none  [the longest x2 5.01 us: body(): lax.all_to_all(synthesised, 'band', split_axis=2, concat_axis=3, tiled=True)]
    reshape x4 -> x0, local copies, waits for them, and re-layouts: 6.25 us -> none  [the longest x1 3.3 us: body(): partial_value.reshape(lev_local, var_count, lat_rows + 1, NLON)]
  transfers between devices with their start and end apart: 7 -> 0, of which waited for: 6 -> 0; matrix products, arithmetic and copies ran while one was open for 3% -> 0% of each run, Pallas kernels for 0% -> 0%
where the time goes in v1:
time: 45.8 us; the launch traced here: 45.5 us
  Pallas kernels  39.9 us (87%)
  local copies, waits for them, and re-layouts  5.6 us (12%)
    pallas_call x1, Pallas kernels, body(): pl.pallas_call(functools.partial(main_kernel, nb, nl, levels), out_shape=...  35.6 us
    pallas_call x1, Pallas kernels, body(): pl.pallas_call(back_kernel, grid=(lev_local,), out_shape=jax.ShapeDtypeSt...  4.3 us
    unnamed x2, local copies, waits for them, and re-layouts  2.92 us
    squeeze x1, local copies, waits for them, and re-layouts, body(): obs_count[0]  1.35 us
    another operation x2, local copies, waits for them, and re-layouts, body(): jnp.tile(quad_weight, 4)[None]  1.33 us

profile of v1, /device:TPU:0, one launch (start us, length us, event | category | flops | bytes accessed | tf_op | source)
XLA Modules:
  0.0 45.5 jit_solution(12683303662704018043)
XLA Ops:
  0.0 0.7 %tile.2 = f32[4,32]{1,0:T(4,128)S(1)} broadcast(f32[32]{0:T(128)} %param.21), dimensions={1} | broadcast | bytes 640 | tf_op jit(solution)/shard_map/tile | solution.py:372
  0.7 0.7 %broadcast_in_dim_tile.3.quad_ref = f32[1,128]{1,0:T(1,128)} reshape(f32[4,32]{1,0:T(4,128)S(1)} %tile.2) | data formatting | bytes 1024 | tf_op jit(solution)/shard_map/broadcast_in_dim;tile | solution.py:372
  1.3 1.3 %copy.14.cnt_ref = s32[8,4]{1,0:T(8,128)} copy(s32[8,4]{0,1:T(4,128)} %bitcast.11) | data formatting | bytes 256 | tf_op jit(solution)/shard_map/squeeze | solution.py:371
  2.7 1.3 %copy.15.cov_ref = f32[4,12,12]{2,1,0:T(8,128)} copy(f32[4,12,12]{2,0,1:T(4,128)} %param.19) | data formatting | bytes 4608 | tf_op args[6]
  4.0 1.6 %copy.16.leg_ref = bf16[4,65,256]{2,1,0:T(8,128)(2,1)} copy(bf16[4,65,256]{2,0,1:T(4,128)(2,1)} %param.22) | data formatting | bytes 266240 | tf_op args[9]
  5.6 35.6 %spectral_covariance.1.spec_ref = f32[32,2,8,128]{3,2,1,0:T(8,128)} custom-call(f32[8,4,128]{2,1,0:T(4,128)} %bitcast.7, f32[8,4,4,128]{3,2,1,0:T(4,128)} %bitcast.6, s32[8,4,128]{2,1,0:T(4,128)} %bitcast.8, s32[8,4,128]{2,1,0:T(4,128)} %bitcast.9, s32[8,4,128]{2,1,0:T(4,128)} %bitcast.10, s32[8,4]{1,0:T(8,128)} %copy.14.cnt_ref, ...), custom_call_target="tpu_custom_call" | custom-call | tf_op jit(solution)/shard_map/spectral_covariance/pallas_call | solution.py:346
  41.2 4.3 %inverse_transform.1 = f32[3,4,32,1440]{3,2,1,0:T(8,128)} custom-call(f32[32,2,8,128]{3,2,1,0:T(8,128)} %spectral_covariance.1.spec_ref, bf16[256,1440]{1,0:T(8,128)(2,1)} %constant.7.clone.high_ref, bf16[256,1440]{1,0:T(8,128)(2,1)} %constant.8.clone.low_ref), custom_call_target="tpu_custom_call" | custom-call | tf_op jit(solution)/shard_map/inverse_transform/pallas_call | solution.py:375

commit v2 on v1

--- a/solution.py
+++ b/solution.py
@@ -61,13 +61,12 @@
     angle = (order[:, None] * np.arange(NLON)[None, :] % NLON) * (2.0 * math.pi / NLON)
     factor = np.where(order == 0, 1.0, 2.0)[:, None] / NLON
     table = factor * np.where(is_sine[:, None] == 1, -np.sin(angle), np.cos(angle))
-    table = np.repeat(table.reshape(-1, 1, 4, NLON), 2, axis=1).reshape(-1, NLON)
     high, low = split_np(table, 2)
-    return high, low
+    return np.concatenate([high, high, low], axis=0)
 
 
 def observation_group(devices):
-    return 4 if devices <= 64 else 1
+    return 8 if devices <= 64 else 1
 
 
 def two(value):
@@ -87,15 +86,16 @@
     nb, nl, levels,
     val_ref, wgt_ref, row_ref, lon_ref, chan_ref, cnt_ref, cov_ref, var_ref, quad_ref, leg_ref, tab_ref,
     out_ref,
-    send1, recv1, send2, recv2, send3, recv3, acc, lpad, xbuf, ssem, rsem1, rsem2, rsem3,
+    send1, recv1, send2, recv2, send3, recv3, acc, lpad, xbuf, tab, quad4, tsem, ssem, rsem1, rsem2, rsem3,
 ):
     devices = nb * nl
     band, lev = lax.axis_index("band"), lax.axis_index("lev")
     me = band * nl + lev
     lev_local = levels // nl
-    var_count = cov_ref.shape[0]
+    var_count = cov_ref.shape[1]
     rows2 = acc.shape[0] // 2
-    orders = leg_ref.shape[1] - 1
+    turned_leg = leg_ref.shape[1] == nl
+    orders = leg_ref.shape[0 if turned_leg else 1] - 1
     nj = leg_ref.shape[2]
     rp = lpad.shape[0]
     tiles = nj // LANES
@@ -103,6 +103,8 @@
     groups = devices // per1
     highest = lax.Precision.HIGHEST
 
+    table_copy = pltpu.make_async_copy(tab_ref, tab, tsem)
+    table_copy.start()
     barrier = pltpu.get_barrier_semaphore()
 
     def greet(k, c):
@@ -112,12 +114,15 @@
 
     lax.fori_loop(1, devices, greet, 0)
 
+    for part in range(4):
+        quad4[:, part * 32:(part + 1) * 32] = quad_ref[...]
+
     slot = lax.broadcasted_iota(jnp.int32, (1, LANES), 1)
 
     def pack(b, c):
         for q in range(nl):
             d = b * nl + q
-            live = slot < cnt_ref[b, q]
+            live = slot < cnt_ref[q, b]
             value = jnp.where(live, val_ref[b, pl.ds(q, 1), :], 0.0)
             send1[d, 0:4, :] = value * wgt_ref[b, q]
             chan = chan_ref[b, pl.ds(q, 1), :]
@@ -128,7 +133,7 @@
             target = (level * var_count + variable) * 32 + row_ref[b, pl.ds(q, 1), :] - b * 32
             send1[d, 4:5, :] = target.astype(jnp.float32)
             send1[d, 5:6, :] = lon_ref[b, pl.ds(q, 1), :].astype(jnp.float32)
-            send1[d, 6:7, :] = quad_ref[...]
+            send1[d, 6:7, :] = quad4[...]
             send1[d, 7:8, :] = jnp.zeros((1, LANES), jnp.float32)
         return c
 
@@ -163,7 +168,12 @@
 
     acc[...] = jnp.zeros_like(acc)
     lpad[...] = jnp.zeros_like(lpad)
-    lpad[0:orders + 1, :] = leg_ref[lev].astype(jnp.float32)
+    if turned_leg:
+        wide = leg_ref[...].astype(jnp.float32)
+        mine = lax.broadcasted_iota(jnp.int32, wide.shape, 1) == lev
+        lpad[0:orders + 1, :] = jnp.sum(jnp.where(mine, wide, 0.0), axis=1)
+    else:
+        lpad[0:orders + 1, :] = leg_ref[lev].astype(jnp.float32)
     leg = lpad[...].astype(jnp.bfloat16)
 
     degree_r = lax.broadcasted_iota(jnp.int32, (orders, rp), 1)
@@ -181,7 +191,7 @@
     same = lax.broadcasted_iota(jnp.int32, (per_v, per_v), 0) % 4 == lax.broadcasted_iota(jnp.int32, (per_v, per_v), 1) % 4
     mixers = []
     for v in range(var_count):
-        left = lax.dot_general(expand, cov_ref[v], NN, precision=highest, preferred_element_type=jnp.float32)
+        left = lax.dot_general(expand, cov_ref[:, v, :], NN, precision=highest, preferred_element_type=jnp.float32)
         full = lax.dot_general(left, expand, NT, precision=highest, preferred_element_type=jnp.float32)
         mixers.append(jnp.where(same, full, 0.0))
 
@@ -201,7 +211,7 @@
             picks.append(jnp.concatenate([a, b, a, b, a, b, jnp.zeros((16, LANES), jnp.bfloat16)], axis=0))
         hot = jnp.concatenate(hots, axis=1)
         pick = jnp.concatenate(picks, axis=1)
-        trig = lax.dot_general(tab_ref[...], pick, NN, preferred_element_type=jnp.float32)
+        trig = lax.dot_general(tab[...], pick, NN, preferred_element_type=jnp.float32)
         ca, sa, cb, sb, ce, se = [trig[i * rows2:(i + 1) * rows2] for i in range(6)]
         here = ca * cb - sa * sb
         east = ca * ce - sa * se
@@ -213,6 +223,7 @@
         acc[...] += dot2(jnp.concatenate([first, second], axis=0), hot, NT)
         return c
 
+    table_copy.wait()
     lax.fori_loop(0, groups, gather_obs, 0)
 
     lane2 = lax.broadcasted_iota(jnp.int32, (rows2, LANES), 1) % 32
@@ -304,7 +315,10 @@
                 part = synth[g * per_v:(g + 1) * per_v, jt * LANES:(jt + 1) * LANES]
                 turned = pltpu.roll(part, 32 * (g - beta) % LANES, 1) if beta != g else part
                 tile = jnp.where(lane_group == g, turned, tile)
-            send3[(4 * jt + beta) * nl:(4 * jt + beta + 1) * nl] = tile.reshape(nl, 2, 8, LANES)
+            tile = tile.reshape(nl, 2, 8, LANES)
+            bands = slice((4 * jt + beta) * nl, (4 * jt + beta + 1) * nl)
+            for t in range(lev_local):
+                send3[bands, t] = tile[:, t // 2, 4 * (t % 2):4 * (t % 2) + 4]
     scatter_out(send3, recv3, 2, rsem3, devices)
     wait_group(recv3, rsem3, 0, devices)
     out_ref[...] = recv3[...]
@@ -313,17 +327,16 @@
     wait_sent(send3, 2)
 
 
-def back_kernel(spec_ref, high_ref, low_ref, out_ref):
-    level = pl.program_id(0)
-    count = spec_ref.shape[0]
-    sub = lax.broadcasted_iota(jnp.int32, (count * 8, LANES), 0) % 8
-    block = spec_ref[:, level // 2].reshape(count * 8, LANES)
-    block = jnp.where(sub // 4 == level % 2, block, 0.0)
-    high, low = two(block.T)
-    both = jnp.concatenate([high, low], axis=0)
-    out = lax.dot_general(both, high_ref[...], NN, preferred_element_type=jnp.float32)
-    rest = lax.dot_general(high, low_ref[...], NN, preferred_element_type=jnp.float32)
-    out = out[:LANES] + out[LANES:] + rest
+def back_kernel(spec_ref, table_ref, out_ref, parts):
+    count, lev_local = spec_ref.shape[:2]
+
+    @pl.when(pl.program_id(0) == 0)
+    def _():
+        for t in range(lev_local):
+            high, low = two(spec_ref[:, t].reshape(count * 4, LANES).T)
+            parts[t * LANES:(t + 1) * LANES, :] = jnp.concatenate([high, low, high], axis=1)
+
+    out = lax.dot_general(parts[...], table_ref[...], NN, preferred_element_type=jnp.float32)
     out_ref[...] = out.reshape(out_ref.shape)
 
 
@@ -343,21 +356,26 @@
         vmem = pl.BlockSpec(memory_space=pltpu.VMEM)
         smem = pl.BlockSpec(memory_space=pltpu.SMEM)
         block = (devices, 2, 8, LANES)
+        ret = (devices, lev_local, 4, LANES)
+        turned_leg = orders <= 64
         spec = pl.pallas_call(
             functools.partial(main_kernel, nb, nl, levels),
-            out_shape=jax.ShapeDtypeStruct(block, jnp.float32),
-            in_specs=[vmem] * 5 + [smem] + [vmem] * 5,
+            out_shape=jax.ShapeDtypeStruct(ret, jnp.float32),
+            in_specs=[vmem] * 5 + [smem] + [vmem] * 4 + [pl.BlockSpec(memory_space=pl.ANY)],
             out_specs=vmem,
             scratch_shapes=[
                 pltpu.VMEM((devices, 8, LANES), jnp.float32),
                 pltpu.VMEM((devices, 8, LANES), jnp.float32),
                 pltpu.VMEM(block, jnp.float32),
                 pltpu.VMEM(block, jnp.float32),
-                pltpu.VMEM(block, jnp.float32),
-                pltpu.VMEM(block, jnp.float32),
+                pltpu.VMEM(ret, jnp.float32),
+                pltpu.VMEM(ret, jnp.float32),
                 pltpu.VMEM((4 * orders, 3 * LANES), jnp.float32),
                 pltpu.VMEM((rp, nj), jnp.float32),
                 pltpu.VMEM((var_count * nl * 16, nj), jnp.float32),
+                pltpu.VMEM((12 * orders, 256), jnp.bfloat16),
+                pltpu.VMEM((1, LANES), jnp.float32),
+                pltpu.SemaphoreType.DMA,
                 pltpu.SemaphoreType.DMA((3,)),
                 pltpu.SemaphoreType.DMA((devices // observation_group(devices),)),
                 pltpu.SemaphoreType.DMA((nj // LANES,)),
@@ -368,23 +386,24 @@
             ),
             name="spectral_covariance",
         )(
-            obs_value[0], obs_weight[0], obs_row[0], obs_lon[0], obs_chan[0], obs_count[0], vert_cov, variance,
-            jnp.tile(quad_weight, 4)[None], legendre, jnp.asarray(point_table(orders)),
+            obs_value[0], obs_weight[0], obs_row[0], obs_lon[0], obs_chan[0], obs_count[0].T, vert_cov.transpose(1, 0, 2), variance,
+            quad_weight[None], legendre.transpose(1, 0, 2) if turned_leg else legendre, jnp.asarray(point_table(orders)),
         )
-        high, low = back_table(orders)
+        table = back_table(orders)
+        width = 768
         return pl.pallas_call(
             back_kernel,
-            grid=(lev_local,),
+            grid=(-(-NLON // width),),
             out_shape=jax.ShapeDtypeStruct((lev_local, var_count, lat_rows, NLON), jnp.float32),
             in_specs=[
-                pl.BlockSpec(block, lambda i: (0, 0, 0, 0)),
-                pl.BlockSpec(high.shape, lambda i: (0, 0)),
-                pl.BlockSpec(low.shape, lambda i: (0, 0)),
+                pl.BlockSpec(ret, lambda i: (0, 0, 0, 0)),
+                pl.BlockSpec((table.shape[0], width), lambda i: (0, i)),
             ],
-            out_specs=pl.BlockSpec((1, var_count, lat_rows, NLON), lambda i: (i, 0, 0, 0)),
+            out_specs=pl.BlockSpec((lev_local, var_count, lat_rows, width), lambda i: (0, 0, 0, i)),
+            scratch_shapes=[pltpu.VMEM((lev_local * LANES, table.shape[0]), jnp.bfloat16)],
             compiler_params=pltpu.CompilerParams(vmem_limit_bytes=56 * 2**20),
             name="inverse_transform",
-        )(spec, jnp.asarray(high), jnp.asarray(low))
+        )(spec, jnp.asarray(table))
 
     placed = (
         P(("band", "lev"), None, None, None),

time: 45.8 us -> 36.3 us (0.79)
  local copies, waits for them, and re-layouts: 5.6 us -> 0 us
  Pallas kernels: 39.9 us -> 36.2 us
    unnamed x2 -> x0, local copies, waits for them, and re-layouts: 2.92 us -> none
    pallas_call x1, Pallas kernels: 35.6 us -> 32.9 us  [body(): pl.pallas_call(functools.partial(main_kernel, nb, nl, levels), out_shape=...]
    squeeze x1 -> x0, local copies, waits for them, and re-layouts: 1.35 us -> none  [body(): obs_count[0]]
    another operation x2 -> x0, local copies, waits for them, and re-layouts: 1.33 us -> none  [body(): jnp.tile(quad_weight, 4)[None]]
    pallas_call x1, Pallas kernels: 4.3 us -> 3.23 us  [body(): pl.pallas_call(back_kernel, grid=(-(-NLON // width),), out_shape=jax.Shap...]
where the time goes in v2:
time: 36.3 us; the launch traced here: 36.2 us
  Pallas kernels  36.2 us (100%)
    pallas_call x1, Pallas kernels, body(): pl.pallas_call(functools.partial(main_kernel, nb, nl, levels), out_shape=...  32.9 us
    pallas_call x1, Pallas kernels, body(): pl.pallas_call(back_kernel, grid=(-(-NLON // width),), out_shape=jax.Shap...  3.23 us

profile of v2, /device:TPU:0, one launch (start us, length us, event | category | flops | bytes accessed | tf_op | source)
XLA Modules:
  0.0 36.2 jit_solution(17041523741000994640)
XLA Ops:
  0.0 32.9 %spectral_covariance.1.spec_ref = f32[32,3,4,128]{3,2,1,0:T(4,128)} custom-call(f32[8,4,128]{2,1,0:T(4,128)} %bitcast.14, f32[8,4,4,128]{3,2,1,0:T(4,128)} %bitcast.12, s32[8,4,128]{2,1,0:T(4,128)} %bitcast.15, s32[8,4,128]{2,1,0:T(4,128)} %bitcast.16, s32[8,4,128]{2,1,0:T(4,128)} %bitcast.17, s32[4,8]{1,0:T(4,128)} %bitcast.18, f32[12,4,12]{2,1,0:T(4,128)} %bitcast.13, ...), custom_call_target="tpu_custom_call" | custom-call | tf_op jit(solution)/shard_map/spectral_covariance/pallas_call | solution.py:361
  32.9 3.2 %inverse_transform.1 = f32[3,4,32,1440]{3,2,1,0:T(8,128)} custom-call(f32[32,3,4,128]{3,2,1,0:T(4,128)} %spectral_covariance.1.spec_ref, bf16[384,1440]{1,0:T(8,128)(2,1)} %constant.5.clone.table_ref), custom_call_target="tpu_custom_call" | custom-call | tf_op jit(solution)/shard_map/inverse_transform/pallas_call | solution.py:394

commit v3 on v2

--- a/solution.py
+++ b/solution.py
@@ -142,7 +142,8 @@
 
     def scatter_out(send, recv, phase, rsem, per):
         def one(k, c):
-            d = lax.rem(me + k, devices)
+            step = jnp.where(k % 2 == 1, (k + 1) // 2, devices - k // 2)
+            d = lax.rem(me + step, devices)
             pltpu.make_async_remote_copy(
                 src_ref=send.at[d],
                 dst_ref=recv.at[me],
@@ -154,7 +155,7 @@
             return c
 
         pltpu.make_async_copy(send.at[me], recv.at[me], rsem.at[me // per]).start()
-        lax.fori_loop(1, devices, one, 0)
+        lax.fori_loop(1, devices, one, 0, unroll=devices <= 64)
 
     def wait_group(recv, rsem, index, per):
         part = recv.at[pl.ds(index * per, per)]

time: 36.3 us -> 35.9 us (0.989)
  Pallas kernels: 36.2 us -> 35.7 us
    pallas_call x1, Pallas kernels: 32.9 us -> 32.5 us  [body(): pl.pallas_call(functools.partial(main_kernel, nb, nl, levels), out_shape=...]
where the time goes in v3:
time: 35.9 us; the launch traced here: 35.7 us
  Pallas kernels  35.7 us (99%)
    pallas_call x1, Pallas kernels, body(): pl.pallas_call(functools.partial(main_kernel, nb, nl, levels), out_shape=...  32.5 us
    pallas_call x1, Pallas kernels, body(): pl.pallas_call(back_kernel, grid=(-(-NLON // width),), out_shape=jax.Shap...  3.23 us

profile of v3, /device:TPU:0, one launch (start us, length us, event | category | flops | bytes accessed | tf_op | source)
XLA Modules:
  0.0 35.7 jit_solution(3946308781272662189)
XLA Ops:
  0.0 32.5 %spectral_covariance.1.spec_ref = f32[32,3,4,128]{3,2,1,0:T(4,128)} custom-call(f32[8,4,128]{2,1,0:T(4,128)} %bitcast.14, f32[8,4,4,128]{3,2,1,0:T(4,128)} %bitcast.12, s32[8,4,128]{2,1,0:T(4,128)} %bitcast.15, s32[8,4,128]{2,1,0:T(4,128)} %bitcast.16, s32[8,4,128]{2,1,0:T(4,128)} %bitcast.17, s32[4,8]{1,0:T(4,128)} %bitcast.18, f32[12,4,12]{2,1,0:T(4,128)} %bitcast.13, ...), custom_call_target="tpu_custom_call" | custom-call | tf_op jit(solution)/shard_map/spectral_covariance/pallas_call | solution.py:362
  32.5 3.2 %inverse_transform.1 = f32[3,4,32,1440]{3,2,1,0:T(8,128)} custom-call(f32[32,3,4,128]{3,2,1,0:T(4,128)} %spectral_covariance.1.spec_ref, bf16[384,1440]{1,0:T(8,128)(2,1)} %constant.5.clone.table_ref), custom_call_target="tpu_custom_call" | custom-call | tf_op jit(solution)/shard_map/inverse_transform/pallas_call | solution.py:395
